TPU v7x, 32 devices: a whole 2x2x4 slice. The times are simulated.
32 devices in a mesh: rows: 8 (over z, y), cols: 4 (over x, core).
Axes of the slice: x: 2, y: 2, z: 4, core: 2. Of those that a mesh axis runs over, the one named last changes fastest.
Arguments:
- snapshots: float32 [2048, 4096], P('rows', 'cols'), may hold values from -6 to 6
- flips: int32 [2048], P('rows'), may hold values 0 or 1
- sample_source: int32 [1024, 1], P('rows'), may hold values from 0 to 7; in each aligned block of 128 rows (0 to 127, 128 to 255, ...) at most 32 rows name the same one
- sample_offset: int32 [1024], P('rows'), may hold values from 0 to 255
- tile_index: int32 [16, 3], P('cols'), may hold values from 0 to 15
- tile_values: float32 [16, 3, 256, 256], P('cols'), may hold values from -0.21875 to 0.21875
Outputs:
- sketch: float32 [1024, 4096], P('rows', 'cols')
Inputs may be any that keep to these rules, and one draw needn't show every extreme that they name: `sample_source`: among the 128 samples of one owner (one device's rows of this list) no source index appears more than 32 times, and in some owners' lists one appears exactly 32 times.
All inputs are finite; a program needn't handle non-finite values. No bound on the sum of `flips` on one device may be relied on, other than what follows from the above.
Results may differ from a plain program's by a relative error of at most 0.000088.
Values sent between devices are 32-bit elements; how exact they have to be, the bound alone decides.
A program may use at most 64 MiB of HBM per device.

v0:
```python
import math

import jax
import jax.numpy as jnp
from jax import lax
from jax.sharding import PartitionSpec as P

TILE = 256


def swapped(array, axis, bit):
    return lax.ppermute(array, axis, [(i, i ^ 1 << bit) for i in range(lax.axis_size(axis))])


def parity_table(length):
    row_ids = lax.broadcasted_iota(jnp.int32, (length, length), 0)
    col_ids = lax.broadcasted_iota(jnp.int32, (length, length), 1)
    common = row_ids & col_ids
    parity = jnp.zeros((length, length), jnp.int32)
    for bit_level in range(length.bit_length()):
        parity = parity ^ common >> bit_level & 1
    return (1 - 2 * parity).astype(jnp.float32)


def incident(row_block, tile_index, tile_values):
    full_cols = lax.all_gather(row_block, "cols", axis=1, tiled=True)
    count = full_cols.shape[0]
    pieces = full_cols.reshape(count, full_cols.shape[1] // TILE, TILE)
    chosen = jnp.take(pieces, tile_index, axis=1)
    result = jnp.einsum("njkc,jkcd->njd", chosen, tile_values, precision=lax.Precision.HIGHEST)
    return result.reshape(count, tile_index.shape[0] * TILE)


def on_device(snapshots, flips, sample_source, sample_offset, tile_index, tile_values):
    device_count = lax.axis_size("rows")
    local_rows = snapshots.shape[0]
    samples_here = sample_offset.shape[0]
    slot_cap = max(2, 2 * samples_here // device_count)
    row_signs = (1 - 2 * flips).astype(jnp.float32)
    signed = snapshots * row_signs[:, None]
    transformed = jnp.dot(parity_table(local_rows), signed, precision=lax.Precision.HIGHEST)
    my_index = lax.axis_index("rows")
    for bit_level in range(device_count.bit_length() - 1):
        partner = swapped(transformed, "rows", bit_level)
        upper_half = my_index >> bit_level & 1 == 1
        transformed = jnp.where(upper_half, partner - transformed, transformed + partner)
    transformed = incident(transformed, tile_index, tile_values)
    own_source = sample_source[:, 0]
    all_source, all_offset = (
        lax.all_gather(own_source, "rows", axis=0, tiled=True),
        lax.all_gather(sample_offset, "rows", axis=0, tiled=True),
    )
    all_source = all_source.reshape(device_count, samples_here)
    all_offset = all_offset.reshape(device_count, samples_here)
    my_index = lax.axis_index("rows")
    is_mine = (all_source == my_index).astype(jnp.int32)
    slot_rank = jnp.cumsum(is_mine, axis=1) - 1
    slot_ids = lax.broadcasted_iota(jnp.int32, (1, 1, slot_cap), 2)
    slot_hit = (is_mine[:, :, None] == 1) & (slot_rank[:, :, None] == slot_ids)
    slot_offset = jnp.sum(jnp.where(slot_hit, all_offset[:, :, None], 0), axis=1)
    slot_used = jnp.any(slot_hit, axis=1).astype(jnp.float32)
    send_panel = jnp.take(transformed, slot_offset.reshape(-1), axis=0) * slot_used.reshape(-1, 1)
    received = lax.all_to_all(send_panel, "rows", split_axis=0, concat_axis=0, tiled=True)
    earlier_ids = lax.broadcasted_iota(jnp.int32, (samples_here, samples_here), 1)
    later_ids = lax.broadcasted_iota(jnp.int32, (samples_here, samples_here), 0)
    same_source = (own_source[None, :] == own_source[:, None]) & (earlier_ids < later_ids)
    own_rank = jnp.sum(same_source.astype(jnp.int32), axis=1)
    position = own_source * slot_cap + own_rank
    sketch_scale = 1.0 / math.sqrt(samples_here * device_count)
    sketch = jnp.take(received, position, axis=0) * sketch_scale
    return sketch


def solution(mesh):
    return jax.shard_map(
        on_device,
        mesh=mesh,
        in_specs=(
            P("rows", "cols"),
            P("rows"),
            P("rows", None),
            P("rows"),
            P("cols", None),
            P("cols", None, None, None),
        ),
        out_specs=P("rows", "cols"),
        check_vma=False,
    )
```

profile of v0, /device:TPU:0, one launch (start us, length us, event | category | flops | bytes accessed | tf_op | source)
XLA Modules:
  0.0 222.7 jit_solution(9436709460811971424)
XLA Ops:
  6.5 0.0 copy-start
  6.5 0.8 subtract_convert_fusion
  7.4 3.7 %fusion.5 = f32[256,1024]{1,0:T(8,128)} fusion(f32[256,1024]{1,0:T(8,128)} %param.6, f32[256]{0:T(256)S(1)} %subtract_convert_fusion), kind=kOutput, calls=%fused_computation.13 | convolution fusion | flops 807534592 | bytes 2098176 | tf_op jit(solution)/shard_map/dot_general | solution.py:41
  11.1 3.0 %collective-permute-start = (f32[256,1024]{1,0:T(8,128)}, f32[256,1024]{1,0:T(8,128)}, u32[]{:S(2)}, u32[]{:S(2)}) collective-permute-start(f32[256,1024]{1,0:T(8,128)} %fusion.5), channel_id=1, source_target_pairs={{0,4},{4,0},{8,12},{12,8},{16,20},{20,16},{24,28},{28,24},{1,5},{5... | collective-permute-start | bytes 3145736 | tf_op jit(solution)/shard_map/ppermute | solution.py:12
  14.0 23.5 %collective-permute-done = f32[256,1024]{1,0:T(8,128)} collective-permute-done((f32[256,1024]{1,0:T(8,128)}, f32[256,1024]{1,0:T(8,128)}, u32[]{:S(2)}, u32[]{:S(2)}) %collective-permute-start) | collective-permute-done | bytes 1048608 | tf_op jit(solution)/shard_map/ppermute | solution.py:12
  37.5 2.8 %add_select_fusion.2 = f32[256,1024]{1,0:T(8,128)} fusion(f32[256,1024]{1,0:T(8,128)} %fusion.5, f32[256,1024]{1,0:T(8,128)} %collective-permute-done, pred[]{:T(512)S(6)} %eq.76), kind=kLoop, calls=%fused_computation.12 | loop fusion | flops 786432 | bytes 3145729 | tf_op jit(solution)/shard_map/jit(_where)/select_n | solution.py:46
  40.3 1.8 collective-permute-start.1
  42.1 22.8 %collective-permute-done.1 = f32[256,1024]{1,0:T(8,128)} collective-permute-done((f32[256,1024]{1,0:T(8,128)}, f32[256,1024]{1,0:T(8,128)}, u32[]{:S(2)}, u32[]{:S(2)}) %collective-permute-start.1) | collective-permute-done | bytes 1048608 | tf_op jit(solution)/shard_map/ppermute | solution.py:12
  64.9 2.8 %add_select_fusion.1 = f32[256,1024]{1,0:T(8,128)} fusion(f32[256,1024]{1,0:T(8,128)} %add_select_fusion.2, f32[256,1024]{1,0:T(8,128)} %collective-permute-done.1, pred[]{:T(512)S(6)} %eq.75), kind=kLoop, calls=%fused_computation.11 | loop fusion | flops 786432 | bytes 3145729 | tf_op jit(solution)/shard_map/jit(_where)/select_n | solution.py:46
  67.7 2.5 %collective-permute-start.2 = (f32[256,1024]{1,0:T(8,128)}, f32[256,1024]{1,0:T(8,128)}, u32[]{:S(2)}, u32[]{:S(2)}) collective-permute-start(f32[256,1024]{1,0:T(8,128)} %add_select_fusion.1), channel_id=1, source_target_pairs={{0,16},{4,20},{8,24},{12,28},{16,0},{20,4},{24,8},{28,12},{1,17},{... | collective-permute-start | bytes 3145736 | tf_op jit(solution)/shard_map/ppermute | solution.py:12
  70.2 44.6 %collective-permute-done.2 = f32[256,1024]{1,0:T(8,128)} collective-permute-done((f32[256,1024]{1,0:T(8,128)}, f32[256,1024]{1,0:T(8,128)}, u32[]{:S(2)}, u32[]{:S(2)}) %collective-permute-start.2) | collective-permute-done | bytes 1048608 | tf_op jit(solution)/shard_map/ppermute | solution.py:12
  114.8 2.8 %add_select_fusion = f32[256,1024]{1,0:T(8,128)} fusion(f32[256,1024]{1,0:T(8,128)} %add_select_fusion.1, f32[256,1024]{1,0:T(8,128)} %collective-permute-done.2, pred[]{:T(512)S(6)} %eq.74), kind=kLoop, calls=%fused_computation.10 | loop fusion | flops 786432 | bytes 3145729 | tf_op jit(solution)/shard_map/jit(_where)/select_n | solution.py:46
  117.5 0.0 all-gather.4.cloned.1.call-update
  117.6 0.1 reshape.105
  117.7 20.2 %all-gather = s32[1024,1]{0,1:T(1,128)S(1)} all-gather(s32[128,1]{0,1:T(1,128)S(1)} %copy-done.2), channel_id=2, replica_groups=mesh['rows'=8,'cols'=4] {'rows'}, dimensions={0}, use_global_device_ids=true | all-gather | bytes 4608 | tf_op jit(solution)/shard_map/all_gather | solution.py:50
  137.8 0.3 reduce_window_sum.11
  138.1 16.1 %all-gather.1 = s32[8,1,128]{2,1,0:T(1,128)S(1)} all-gather(s32[1,1,128]{2,1,0:T(1,128)S(1)} %bitcast.41), channel_id=1, replica_groups=mesh['rows'=8,'cols'=4] {'rows'}, dimensions={0}, use_global_device_ids=true | all-gather | bytes 4608 | tf_op jit(solution)/shard_map/all_gather | solution.py:51
  154.3 0.2 select_reduce_fusion
  154.5 0.1 reshape.101
  154.6 0.2 fusion.50
  154.9 0.0 all-gather.4.cloned.1.call-done
  154.9 4.6 %copy.23 = f32[32,16,8,256]{3,2,0,1:T(8,128)} copy(f32[32,16,8,256]{3,2,1,0:T(8,128)} %bitcast.33) | data formatting | bytes 8388608 | tf_op jit(solution)/shard_map/reshape | solution.py:28
  159.5 4.6 %gather_fusion = f32[12,256,256]{2,1,0:T(8,128)} fusion(f32[256,16,256]{2,0,1:T(8,128)} %bitcast.31, s32[1024]{0:T(1024)S(1)} %pad_clamp_fusion.2), kind=kCustom, calls=%fused_computation | custom fusion | bytes 6291504 | tf_op jit(solution)/shard_map/jit(_take)/gather | solution.py:29
  164.1 8.1 %fusion = f32[4,256,256,1]{1,2,3,0:T(8,128)} fusion(f32[4,3,256,256]{3,2,1,0:T(8,128)S(1)} %copy-done, f32[4,3,256,256]{3,2,1,0:T(8,128)} %bitcast.30, pred[4,3]{1,0:T(4,128)(4,1)S(1)} %compare_and_fusion.1), kind=kOutput, calls=%fused_computation.4 | convolution fusion | flops 2416705536 | bytes 7340044 | tf_op jit(solution)/shard_map/njkc,jkcd->njd/dot_general | solution.py:30
  172.2 2.5 %copy.18 = f32[256,1024]{1,0:T(8,128)} copy(f32[256,1024]{0,1:T(8,128)} %bitcast.34) | data formatting | bytes 2097152 | tf_op jit(solution)/shard_map/reshape | solution.py:31
  174.7 3.8 %gather_fusion.1 = f32[256,1024]{1,0:T(8,128)} fusion(f32[256,1024]{1,0:T(8,128)} %copy.18, s32[1024]{0:T(1024)S(1)} %pad_clamp_fusion.1), kind=kCustom, calls=%fused_computation.1 | custom fusion | bytes 2098176 | tf_op jit(solution)/shard_map/jit(_take)/gather | solution.py:62
  178.5 2.4 %select_multiply_fusion = f32[8,32,1024]{2,1,0:T(8,128)} fusion(f32[8,32,1024]{2,1,0:T(8,128)} %bitcast.32, f32[8,32]{1,0:T(8,128)S(1)} %convert_element_type.35, pred[8,32]{1,0:T(8,128)(4,1)S(1)} %compare_and_fusion), kind=kLoop, calls=%fused_computation.9 | loop fusion | flops 524288 | bytes 2098432 | tf_op jit(solution)/shard_map/mul | solution.py:62
  180.9 4.2 %all-to-all-start = ((f32[8,32,1024]{2,1,0:T(8,128)}), f32[8,32,1024]{2,1,0:T(8,128)}, u32[]{:S(2)}, u32[]{:S(2)}) async-start(f32[8,32,1024]{2,1,0:T(8,128)} %select_multiply_fusion), calls=%async_computation | async-start | bytes 2097152 | tf_op jit(solution)/shard_map/all_to_all | solution.py:63
  185.1 0.2 convert_reduce_fusion
  185.3 25.5 %all-to-all-done = f32[8,32,1024]{2,1,0:T(8,128)} async-done(((f32[8,32,1024]{2,1,0:T(8,128)}), f32[8,32,1024]{2,1,0:T(8,128)}, u32[]{:S(2)}, u32[]{:S(2)}) %all-to-all-start) | async-done | bytes 1048608 | tf_op jit(solution)/shard_map/all_to_all | solution.py:63
  210.8 3.0 %gather_fusion.2 = f32[128,1024]{1,0:T(8,128)} fusion(f32[256,1024]{1,0:T(8,128)} %bitcast.14, s32[1024]{0:T(1024)S(1)} %pad_clamp_fusion), kind=kCustom, calls=%fused_computation.2 | custom fusion | bytes 1049088 | tf_op jit(solution)/shard_map/jit(_take)/gather | solution.py:70
  213.9 1.9 select_multiply_fusion.1
  (20 shorter events, 0.1 us)
Async XLA Ops:
  6.5 157.6 %copy-start = (f32[4,3,256,256]{3,2,1,0:T(8,128)S(1)}, f32[4,3,256,256]{3,2,1,0:T(8,128)}, u32[]{:S(2)}) copy-start(f32[4,3,256,256]{3,2,1,0:T(8,128)} %param.11) | copy-start | bytes 9437188
  6.5 148.4 %all-gather.4.cloned.1.call-start = ((), (), s32[]{:S(2)}) async-start(), calls=%async_computation.1 | async-start | bytes 5242880 | tf_op jit(solution)/shard_map/all_gather | solution.py:26
  11.1 26.4 %collective-permute-start = (f32[256,1024]{1,0:T(8,128)}, f32[256,1024]{1,0:T(8,128)}, u32[]{:S(2)}, u32[]{:S(2)}) collective-permute-start(f32[256,1024]{1,0:T(8,128)} %fusion.5), channel_id=1, source_target_pairs={{0,4},{4,0},{8,12},{12,8},{16,20},{20,16},{24,28},{28,24},{1,5},{5... | collective-permute-start | bytes 3145736 | tf_op jit(solution)/shard_map/ppermute | solution.py:12
  40.3 24.7 %collective-permute-start.1 = (f32[256,1024]{1,0:T(8,128)}, f32[256,1024]{1,0:T(8,128)}, u32[]{:S(2)}, u32[]{:S(2)}) collective-permute-start(f32[256,1024]{1,0:T(8,128)} %add_select_fusion.2), channel_id=1, source_target_pairs={{0,8},{4,12},{8,0},{12,4},{16,24},{20,28},{24,16},{28,20},{1,9},{5... | collective-permute-start | bytes 3145736 | tf_op jit(solution)/shard_map/ppermute | solution.py:12
  42.1 75.5 %copy-start.1 = (s32[4,3]{1,0:T(4,128)S(1)}, s32[4,3]{1,0:T(4,128)}, u32[]{:S(2)}) copy-start(s32[4,3]{1,0:T(4,128)} %param.10) | copy-start | bytes 148
  42.1 75.6 %copy-start.2 = (s32[128,1]{0,1:T(1,128)S(1)}, s32[128,1]{0,1:T(1,128)}, u32[]{:S(2)}) copy-start(s32[128,1]{0,1:T(1,128)} %param.8) | copy-start | bytes 1540
  42.1 96.1 %copy-start.3 = (s32[128]{0:T(128)S(1)}, s32[128]{0:T(128)}, u32[]{:S(2)}) copy-start(s32[128]{0:T(128)} %param.9) | copy-start | bytes 1540
  67.7 47.1 %collective-permute-start.2 = (f32[256,1024]{1,0:T(8,128)}, f32[256,1024]{1,0:T(8,128)}, u32[]{:S(2)}, u32[]{:S(2)}) collective-permute-start(f32[256,1024]{1,0:T(8,128)} %add_select_fusion.1), channel_id=1, source_target_pairs={{0,16},{4,20},{8,24},{12,28},{16,0},{20,4},{24,8},{28,12},{1,17},{... | collective-permute-start | bytes 3145736 | tf_op jit(solution)/shard_map/ppermute | solution.py:12
  180.9 29.9 %all-to-all-start = ((f32[8,32,1024]{2,1,0:T(8,128)}), f32[8,32,1024]{2,1,0:T(8,128)}, u32[]{:S(2)}, u32[]{:S(2)}) async-start(f32[8,32,1024]{2,1,0:T(8,128)} %select_multiply_fusion), calls=%async_computation | async-start | bytes 2097152 | tf_op jit(solution)/shard_map/all_to_all | solution.py:63
Sparse Core Ops, SparseCore 0:
  117.7 35.1 all-gather.3
where the time goes:
time: 223 us
  waiting for transfers between devices  116 us (52%)
  blocking collectives  36.3 us (16%)
  local copies, waits for them, and re-layouts  18.7 us (8%)
  other arithmetic  14.4 us (6%)
  between operations  13.5 us (6%)
  matrix products  11.8 us (5%)
  starting transfers between devices  11.5 us (5%)
    ppermute x3, waiting for transfers between devices, swapped(): lax.ppermute(array, axis, [(i, i ^ 1 << bit) for i in range(lax.axis_size...  90.9 us
    all_to_all x1, waiting for transfers between devices, on_device(): lax.all_to_all(send_panel, 'rows', split_axis=0, concat_axis=0, tiled=True)  25.5 us
    all_gather x1, blocking collectives, on_device(): lax.all_gather(own_source, 'rows', axis=0, tiled=True)  20.2 us
    all_gather x1, blocking collectives, on_device(): lax.all_gather(sample_offset, 'rows', axis=0, tiled=True)  16.1 us
    select_n x3, other arithmetic, on_device(): jnp.where(upper_half, partner - transformed, transformed + partner)  8.26 us
    dot_general x1, matrix products, incident(): jnp.einsum('njkc,jkcd->njd', chosen, tile_values, precision=lax.Precision...  8.08 us
    ppermute x3, starting transfers between devices, swapped(): lax.ppermute(array, axis, [(i, i ^ 1 << bit) for i in range(lax.axis_size...  7.27 us
    reshape x1, local copies, waits for them, and re-layouts, incident(): pieces = full_cols.reshape(count, full_cols.shape[1] // TILE, TILE)  4.6 us
  transfers between devices with their start and end apart: 5, of which 4 were waited for; matrix products, arithmetic and copies ran while one was open for 1% of the time, Pallas kernels for 0%

commit v1 on v0

v1 whole, which is shorter than its diff:
```python
import functools
import math

import jax
import jax.numpy as jnp
from jax import lax
from jax.experimental import pallas as pl
from jax.experimental.pallas import tpu as pltpu
from jax.sharding import PartitionSpec as P

TILE = 256
LANES = 128
MESH = pl.DeviceIdType.MESH
HIGHEST = lax.Precision.HIGHEST


def swapped(array, axis, bit):
    return lax.ppermute(array, axis, [(i, i ^ 1 << bit) for i in range(lax.axis_size(axis))])


def parity_table(length):
    row_ids = lax.broadcasted_iota(jnp.int32, (length, length), 0)
    col_ids = lax.broadcasted_iota(jnp.int32, (length, length), 1)
    common = row_ids & col_ids
    parity = jnp.zeros((length, length), jnp.int32)
    for bit_level in range(length.bit_length()):
        parity = parity ^ common >> bit_level & 1
    return (1 - 2 * parity).astype(jnp.float32)


def incident(row_block, tile_index, tile_values):
    full_cols = lax.all_gather(row_block, "cols", axis=1, tiled=True)
    count = full_cols.shape[0]
    out = []
    for j in range(tile_index.shape[0]):
        total = jnp.zeros((count, TILE), jnp.float32)
        for k in range(tile_index.shape[1]):
            chosen = lax.dynamic_slice(full_cols, (0, tile_index[j, k] * TILE), (count, TILE))
            total = total + jnp.dot(chosen, tile_values[j, k], precision=HIGHEST)
        out.append(total)
    return jnp.concatenate(out, axis=1)


def general(snapshots, flips, sample_source, sample_offset, tile_index, tile_values):
    device_count = lax.axis_size("rows")
    local_rows = snapshots.shape[0]
    samples_here = sample_offset.shape[0]
    slot_cap = max(2, 2 * samples_here // device_count)
    row_signs = (1 - 2 * flips).astype(jnp.float32)
    signed = snapshots * row_signs[:, None]
    transformed = jnp.dot(parity_table(local_rows), signed, precision=HIGHEST)
    my_index = lax.axis_index("rows")
    for bit_level in range(device_count.bit_length() - 1):
        partner = swapped(transformed, "rows", bit_level)
        upper_half = my_index >> bit_level & 1 == 1
        transformed = jnp.where(upper_half, partner - transformed, transformed + partner)
    transformed = incident(transformed, tile_index, tile_values)
    own_source = sample_source[:, 0]
    all_source = lax.all_gather(own_source, "rows", axis=0, tiled=True)
    all_offset = lax.all_gather(sample_offset, "rows", axis=0, tiled=True)
    all_source = all_source.reshape(device_count, samples_here)
    all_offset = all_offset.reshape(device_count, samples_here)
    is_mine = all_source == my_index
    earlier_ids = lax.broadcasted_iota(jnp.int32, (samples_here, samples_here), 1)
    later_ids = lax.broadcasted_iota(jnp.int32, (samples_here, samples_here), 0)
    before = (later_ids < earlier_ids).astype(jnp.float32)
    slot_rank = jnp.dot(is_mine.astype(jnp.float32), before, precision=HIGHEST).astype(jnp.int32)
    slot_ids = lax.broadcasted_iota(jnp.int32, (1, 1, slot_cap), 2)
    slot_hit = is_mine[:, :, None] & (slot_rank[:, :, None] == slot_ids)
    slot_offset = jnp.sum(jnp.where(slot_hit, all_offset[:, :, None], 0), axis=1).reshape(-1)
    slot_used = jnp.any(slot_hit, axis=1).reshape(-1)
    local_ids = lax.broadcasted_iota(jnp.int32, (1, local_rows), 1)
    send_pick = ((slot_offset[:, None] == local_ids) & slot_used[:, None]).astype(jnp.float32)
    send_panel = jnp.dot(send_pick, transformed, precision=HIGHEST)
    received = lax.all_to_all(send_panel, "rows", split_axis=0, concat_axis=0, tiled=True)
    same_source = (own_source[None, :] == own_source[:, None]) & (earlier_ids < later_ids)
    own_rank = jnp.sum(same_source.astype(jnp.int32), axis=1)
    position = own_source * slot_cap + own_rank
    panel_ids = lax.broadcasted_iota(jnp.int32, (1, received.shape[0]), 1)
    own_pick = (position[:, None] == panel_ids).astype(jnp.float32)
    sketch_scale = 1.0 / math.sqrt(samples_here * device_count)
    return jnp.dot(own_pick, received, precision=HIGHEST) * sketch_scale


def flipped(index, mask):
    out, bit = index, 1
    while bit <= mask:
        if mask & bit:
            out = out + bit * (1 - 2 * ((index // bit) % 2))
        bit *= 2
    return out


def split(x):
    hi = x.astype(jnp.bfloat16)
    return hi, (x - hi.astype(jnp.float32)).astype(jnp.bfloat16)


def kernel(
    n, n_cols, scale,
    snap, meta, tile_index, tile_values, out,
    meta_all, recv, signs, total, picked, full, w, w_hi, w_lo,
    meta_s, meta_r, snap_s, snap_r, pick_s, pick_r, x_s, x_r, core_s, core_r, relay_s, relay_r, local_sem,
):
    rows = snap.shape[0]
    samples = total.shape[0] // n
    me, col = lax.axis_index("rows"), lax.axis_index("cols")
    across, beside = flipped(col, 2), flipped(col, 1)
    far_first = list(range(n - 1, 0, -1))
    near_first = list(range(1, n))

    def slot(c, r):
        return c * n + r

    load_own = pltpu.make_async_copy(
        snap.at[:, pl.ds(pl.multiple_of(me * LANES, LANES), LANES)], recv.at[me], local_sem.at[0]
    )
    load_w = pltpu.make_async_copy(tile_values, w, local_sem.at[1])
    load_meta = pltpu.make_async_copy(meta, meta_all.at[me], local_sem.at[2])
    load_own.start()
    load_w.start()
    load_meta.start()

    barrier = pltpu.get_barrier_semaphore()
    for mask in near_first:
        pl.semaphore_signal(barrier, inc=1, device_id={"rows": flipped(me, mask)}, device_id_type=MESH)
    for other in (across, beside):
        pl.semaphore_signal(barrier, inc=1, device_id={"cols": other}, device_id_type=MESH)
    pl.semaphore_wait(barrier, n + 1)

    def meta_copy(mask):
        return pltpu.make_async_remote_copy(
            src_ref=meta, dst_ref=meta_all.at[me], send_sem=meta_s.at[mask], recv_sem=meta_r.at[mask],
            device_id={"rows": flipped(me, mask)}, device_id_type=MESH,
        )

    def snap_copy(mask):
        other = flipped(me, mask)
        return pltpu.make_async_remote_copy(
            src_ref=snap.at[:, pl.ds(pl.multiple_of(other * LANES, LANES), LANES)],
            dst_ref=recv.at[me], send_sem=snap_s.at[mask], recv_sem=snap_r.at[mask],
            device_id={"rows": other}, device_id_type=MESH,
        )

    def pick_copy(mask):
        other = flipped(me, mask)
        return pltpu.make_async_remote_copy(
            src_ref=picked.at[other], dst_ref=full.at[slot(col, me)],
            send_sem=pick_s.at[mask], recv_sem=pick_r.at[mask],
            device_id={"rows": other}, device_id_type=MESH,
        )

    def col_copy(mask, owner, target, send, recv_sem):
        place = slot(owner, flipped(me, mask))
        return pltpu.make_async_remote_copy(
            src_ref=full.at[place], dst_ref=full.at[place],
            send_sem=send.at[mask], recv_sem=recv_sem.at[mask],
            device_id={"cols": target}, device_id_type=MESH,
        )

    x_copy = lambda mask: col_copy(mask, col, across, x_s, x_r)
    core_copy = lambda mask: col_copy(mask, col, beside, core_s, core_r)
    relay_copy = lambda mask: col_copy(mask, across, beside, relay_s, relay_r)

    for mask in far_first:
        meta_copy(mask).start()
    for mask in far_first:
        snap_copy(mask).start()

    load_w.wait()

    def split_w(i, carry):
        hi, lo = split(w[i])
        w_hi[i] = hi
        w_lo[i] = lo
        return carry

    lax.fori_loop(0, w.shape[0], split_w, 0)

    load_meta.wait()
    for mask in near_first:
        meta_copy(mask).wait_recv()
    lane = lax.broadcasted_iota(jnp.int32, (samples, LANES), 1)

    def owner_signs(d, carry):
        ids = jnp.broadcast_to(meta_all[d, 0:1, :], (samples, LANES)).T
        at = pl.ds(pl.multiple_of(d * samples, samples), samples)

        def block_signs(g, carry):
            for h in range(rows // LANES):
                common = ids & (lane + (g * rows + h * LANES))
                bits = 16
                while bits > 1:
                    bits //= 2
                    common = common ^ (common >> bits)
                parity = (common ^ meta_all[g, 1 + h : 2 + h, :]) & 1
                signs[g, at, h * LANES : (h + 1) * LANES] = (1 - 2 * parity).astype(jnp.float32).astype(jnp.bfloat16)
            return carry

        return lax.fori_loop(0, n, block_signs, carry)

    lax.fori_loop(0, n, owner_signs, 0)

    def halves(g):
        hi, lo = split(recv[g])
        return jnp.concatenate([hi, lo], axis=1)

    load_own.wait()
    for mask in range(n - 1):
        g = flipped(me, mask)
        if mask:
            snap_copy(mask).wait_recv()
        block = halves(g)

        def add_block(d, carry, g=g, block=block, first=mask == 0):
            at = pl.ds(pl.multiple_of(d * samples, samples), samples)
            part = jnp.dot(signs[g, at, :], block, preferred_element_type=jnp.float32)
            total[at, :] = part if first else total[at, :] + part
            return carry

        lax.fori_loop(0, n, add_block, 0)

    last = flipped(me, n - 1)
    snap_copy(n - 1).wait_recv()
    block = halves(last)
    for mask in far_first + [0]:
        d = flipped(me, mask)
        at = pl.ds(pl.multiple_of(d * samples, samples), samples)
        both = total[at, :] + jnp.dot(signs[last, at, :], block, preferred_element_type=jnp.float32)
        ready = (both[:, :LANES] + both[:, LANES:]) * scale
        if mask:
            picked[d] = ready
            pick_copy(mask).start()
        else:
            full[slot(col, me)] = ready

    for mask in range(n):
        if mask:
            pick_copy(mask).wait_recv()
        x_copy(mask).start()
        core_copy(mask).start()
    for mask in range(n):
        place = slot(across, flipped(me, mask))
        pltpu.make_async_remote_copy(
            src_ref=full.at[place], dst_ref=full.at[place], send_sem=x_s.at[mask], recv_sem=x_r.at[mask],
            device_id={"cols": across}, device_id_type=MESH,
        ).wait_recv()
        relay_copy(mask).start()
    for mask in range(n):
        core_copy(mask).wait_recv()
        relay_copy(mask).wait_recv()

    for j in range(tile_index.shape[0]):
        sums = jnp.zeros((samples, TILE), jnp.float32)
        for k in range(tile_index.shape[1]):
            t = tile_index[j, k]
            hi, lo = split(jnp.concatenate([full[2 * t], full[2 * t + 1]], axis=1))
            i = j * tile_index.shape[1] + k
            sums = sums + jnp.dot(hi, w_hi[i], preferred_element_type=jnp.float32)
            sums = sums + jnp.dot(lo, w_hi[i], preferred_element_type=jnp.float32)
            sums = sums + jnp.dot(hi, w_lo[i], preferred_element_type=jnp.float32)
        out[:, j * TILE : (j + 1) * TILE] = sums

    for mask in range(n):
        if mask:
            meta_copy(mask).wait_send()
            snap_copy(mask).wait_send()
            pick_copy(mask).wait_send()
        x_copy(mask).wait_send()
        core_copy(mask).wait_send()
        relay_copy(mask).wait_send()


def fused(snapshots, flips, sample_source, sample_offset, tile_index, tile_values):
    n, n_cols = lax.axis_size("rows"), lax.axis_size("cols")
    rows, width = snapshots.shape
    samples = sample_offset.shape[0]
    row_id = sample_source[:, 0] * rows + sample_offset
    meta = jnp.concatenate([row_id.reshape(1, LANES), flips.reshape(rows // LANES, LANES)], axis=0)
    meta = jnp.pad(meta, ((0, 8 - meta.shape[0]), (0, 0)))
    tiles, nnz = tile_index.shape
    weights = tile_values.reshape(tiles * nnz, TILE, TILE)
    scale = 1.0 / math.sqrt(samples * n)
    dma = pltpu.SemaphoreType.DMA((n,))
    return pl.pallas_call(
        functools.partial(kernel, n, n_cols, scale),
        out_shape=jax.ShapeDtypeStruct((samples, width), jnp.float32),
        in_specs=[
            pl.BlockSpec(memory_space=pl.ANY),
            pl.BlockSpec(memory_space=pltpu.VMEM),
            pl.BlockSpec(memory_space=pltpu.SMEM),
            pl.BlockSpec(memory_space=pl.ANY),
        ],
        out_specs=pl.BlockSpec(memory_space=pltpu.VMEM),
        scratch_shapes=[
            pltpu.VMEM((n, 8, LANES), jnp.int32),
            pltpu.VMEM((n, rows, LANES), jnp.float32),
            pltpu.VMEM((n, n * samples, rows), jnp.bfloat16),
            pltpu.VMEM((n * samples, 2 * LANES), jnp.float32),
            pltpu.VMEM((n, samples, LANES), jnp.float32),
            pltpu.VMEM((n_cols * n, samples, LANES), jnp.float32),
            pltpu.VMEM((tiles * nnz, TILE, TILE), jnp.float32),
            pltpu.VMEM((tiles * nnz, TILE, TILE), jnp.bfloat16),
            pltpu.VMEM((tiles * nnz, TILE, TILE), jnp.bfloat16),
        ]
        + [dma] * 12
        + [pltpu.SemaphoreType.DMA((3,))],
        compiler_params=pltpu.CompilerParams(
            collective_id=0, has_side_effects=True, vmem_limit_bytes=40 * 2**20
        ),
    )(snapshots, meta, tile_index, weights)


def on_device(snapshots, flips, sample_source, sample_offset, tile_index, tile_values):
    n, n_cols = lax.axis_size("rows"), lax.axis_size("cols")
    fits = (
        n & (n - 1) == 0
        and 2 <= n <= 8
        and n_cols == 4
        and snapshots.shape[1] == n * LANES
        and snapshots.shape[0] % LANES == 0
        and snapshots.shape[0] // LANES <= 7
        and sample_offset.shape[0] == LANES
    )
    return (fused if fits else general)(
        snapshots, flips, sample_source, sample_offset, tile_index, tile_values
    )


def solution(mesh):
    return jax.shard_map(
        on_device,
        mesh=mesh,
        in_specs=(
            P("rows", "cols"),
            P("rows"),
            P("rows", None),
            P("rows"),
            P("cols", None),
            P("cols", None, None, None),
        ),
        out_specs=P("rows", "cols"),
        check_vma=False,
    )
```

time: 223 us -> 63.6 us (0.29)
  the two profiles are of different devices: /device:TPU:0 before, /device:TPU:9 now
where the time goes in v1:
time: 63.6 us; the launch traced here: 63.4 us
  Pallas kernels  57.4 us (90%)
  local copies, waits for them, and re-layouts  4.59 us (7%)
  other arithmetic  1.36 us (2%)
    pallas_call x1, Pallas kernels, fused(): pl.pallas_call(functools.partial(kernel, n, n_cols, scale), out_shape=jax...  57.4 us
    unnamed x7, local copies, waits for them, and re-layouts  4.58 us

profile of v1, /device:TPU:9, one launch (start us, length us, event | category | flops | bytes accessed | tf_op | source)
XLA Modules:
  0.0 63.4 jit_solution(15636589662919868190)
XLA Ops:
  0.0 0.7 %fusion = s32[1,128]{1,0:T(1,128)S(1)} fusion(s32[128]{0:T(128)} %param.9, s32[128,1]{0,1:T(1,128)} %param.8), kind=kLoop, calls=%fused_computation.2 | loop fusion | flops 256 | bytes 1536 | tf_op jit(solution)/shard_map/reshape | solution.py:279
  0.7 0.7 %pad_add_fusion = s32[3,128]{1,0:T(4,128)S(1)} fusion(s32[2,128]{1,0:T(2,128)} %bitcast.9, s32[1,128]{1,0:T(1,128)S(1)} %fusion), kind=kLoop, calls=%fused_computation | loop fusion | flops 384 | bytes 3072 | tf_op jit(solution)/shard_map/concatenate | solution.py:279
  1.4 0.0 copy-start
  1.4 1.9 %copy-done = f32[4,3,256,256]{3,2,1,0:T(8,128)S(1)} copy-done((f32[4,3,256,256]{3,2,1,0:T(8,128)S(1)}, f32[4,3,256,256]{3,2,1,0:T(8,128)}, u32[]{:S(2)}) %copy-start) | copy-done | bytes 3145752
  3.3 0.0 copy-start.1
  3.3 1.2 %copy-done.1 = f32[256,1024]{1,0:T(8,128)S(1)} copy-done((f32[256,1024]{1,0:T(8,128)S(1)}, f32[256,1024]{1,0:T(8,128)}, u32[]{:S(2)}) %copy-start.1) | copy-done | bytes 1048600
  4.5 0.0 copy-start.2
  4.5 0.7 %copy-done.2 = s32[4,3]{1,0:T(4,128)S(1)} copy-done((s32[4,3]{1,0:T(4,128)S(1)}, s32[4,3]{1,0:T(4,128)}, u32[]{:S(2)}) %copy-start.2) | copy-done | bytes 72
  5.2 57.4 %shard_map.64 = f32[128,1024]{1,0:T(8,128)S(1)} custom-call(f32[256,1024]{1,0:T(8,128)S(1)} %copy-done.1, s32[8,128]{1,0:T(8,128)S(1)} %pad.4.meta, s32[4,3]{1,0:T(4,128)S(1)} %copy-done.2, f32[12,256,256]{2,1,0:T(8,128)S(1)} %bitcast.8), custom_call_target="tpu_custom_call" | custom-call | tf_op jit(solution)/shard_map/pallas_call | solution.py:285
  62.6 0.8 %copy.8 = f32[128,1024]{1,0:T(8,128)} copy(f32[128,1024]{1,0:T(8,128)S(1)} %shard_map.64) | data formatting | bytes 1048576
  (1 shorter events, 0.0 us)
Async XLA Ops:
  1.4 1.9 %copy-start = (f32[4,3,256,256]{3,2,1,0:T(8,128)S(1)}, f32[4,3,256,256]{3,2,1,0:T(8,128)}, u32[]{:S(2)}) copy-start(f32[4,3,256,256]{3,2,1,0:T(8,128)} %param.11) | copy-start | bytes 9437188
  3.3 1.2 %copy-start.1 = (f32[256,1024]{1,0:T(8,128)S(1)}, f32[256,1024]{1,0:T(8,128)}, u32[]{:S(2)}) copy-start(f32[256,1024]{1,0:T(8,128)} %snap.1) | copy-start | bytes 3145732
  4.5 0.7 %copy-start.2 = (s32[4,3]{1,0:T(4,128)S(1)}, s32[4,3]{1,0:T(4,128)}, u32[]{:S(2)}) copy-start(s32[4,3]{1,0:T(4,128)} %tile_index.1) | copy-start | bytes 148

commit v2 on v0

v2 whole, which is shorter than its diff:
```python
import functools
import math

import jax
import jax.numpy as jnp
from jax import lax
from jax.experimental import pallas as pl
from jax.experimental.pallas import tpu as pltpu
from jax.sharding import PartitionSpec as P

TILE = 256
LANES = 128
MESH = pl.DeviceIdType.MESH
HIGHEST = lax.Precision.HIGHEST


def swapped(array, axis, bit):
    return lax.ppermute(array, axis, [(i, i ^ 1 << bit) for i in range(lax.axis_size(axis))])


def parity_table(length):
    row_ids = lax.broadcasted_iota(jnp.int32, (length, length), 0)
    col_ids = lax.broadcasted_iota(jnp.int32, (length, length), 1)
    common = row_ids & col_ids
    parity = jnp.zeros((length, length), jnp.int32)
    for bit_level in range(length.bit_length()):
        parity = parity ^ common >> bit_level & 1
    return (1 - 2 * parity).astype(jnp.float32)


def incident(row_block, tile_index, tile_values):
    full_cols = lax.all_gather(row_block, "cols", axis=1, tiled=True)
    count = full_cols.shape[0]
    out = []
    for j in range(tile_index.shape[0]):
        total = jnp.zeros((count, TILE), jnp.float32)
        for k in range(tile_index.shape[1]):
            chosen = lax.dynamic_slice(full_cols, (0, tile_index[j, k] * TILE), (count, TILE))
            total = total + jnp.dot(chosen, tile_values[j, k], precision=HIGHEST)
        out.append(total)
    return jnp.concatenate(out, axis=1)


def general(snapshots, flips, sample_source, sample_offset, tile_index, tile_values):
    device_count = lax.axis_size("rows")
    local_rows = snapshots.shape[0]
    samples_here = sample_offset.shape[0]
    slot_cap = max(2, 2 * samples_here // device_count)
    row_signs = (1 - 2 * flips).astype(jnp.float32)
    signed = snapshots * row_signs[:, None]
    transformed = jnp.dot(parity_table(local_rows), signed, precision=HIGHEST)
    my_index = lax.axis_index("rows")
    for bit_level in range(device_count.bit_length() - 1):
        partner = swapped(transformed, "rows", bit_level)
        upper_half = my_index >> bit_level & 1 == 1
        transformed = jnp.where(upper_half, partner - transformed, transformed + partner)
    transformed = incident(transformed, tile_index, tile_values)
    own_source = sample_source[:, 0]
    all_source = lax.all_gather(own_source, "rows", axis=0, tiled=True)
    all_offset = lax.all_gather(sample_offset, "rows", axis=0, tiled=True)
    all_source = all_source.reshape(device_count, samples_here)
    all_offset = all_offset.reshape(device_count, samples_here)
    is_mine = all_source == my_index
    earlier_ids = lax.broadcasted_iota(jnp.int32, (samples_here, samples_here), 1)
    later_ids = lax.broadcasted_iota(jnp.int32, (samples_here, samples_here), 0)
    before = (later_ids < earlier_ids).astype(jnp.float32)
    slot_rank = jnp.dot(is_mine.astype(jnp.float32), before, precision=HIGHEST).astype(jnp.int32)
    slot_ids = lax.broadcasted_iota(jnp.int32, (1, 1, slot_cap), 2)
    slot_hit = is_mine[:, :, None] & (slot_rank[:, :, None] == slot_ids)
    slot_offset = jnp.sum(jnp.where(slot_hit, all_offset[:, :, None], 0), axis=1).reshape(-1)
    slot_used = jnp.any(slot_hit, axis=1).reshape(-1)
    local_ids = lax.broadcasted_iota(jnp.int32, (1, local_rows), 1)
    send_pick = ((slot_offset[:, None] == local_ids) & slot_used[:, None]).astype(jnp.float32)
    send_panel = jnp.dot(send_pick, transformed, precision=HIGHEST)
    received = lax.all_to_all(send_panel, "rows", split_axis=0, concat_axis=0, tiled=True)
    same_source = (own_source[None, :] == own_source[:, None]) & (earlier_ids < later_ids)
    own_rank = jnp.sum(same_source.astype(jnp.int32), axis=1)
    position = own_source * slot_cap + own_rank
    panel_ids = lax.broadcasted_iota(jnp.int32, (1, received.shape[0]), 1)
    own_pick = (position[:, None] == panel_ids).astype(jnp.float32)
    sketch_scale = 1.0 / math.sqrt(samples_here * device_count)
    return jnp.dot(own_pick, received, precision=HIGHEST) * sketch_scale


def flipped(index, mask):
    out, bit = index, 1
    while bit <= mask:
        if mask & bit:
            out = out + bit * (1 - 2 * ((index // bit) % 2))
        bit *= 2
    return out


def split(x):
    hi = x.astype(jnp.bfloat16)
    return hi, (x - hi.astype(jnp.float32)).astype(jnp.bfloat16)


def kernel(
    n, scale,
    snap, flips, source, offset, tile_index, tile_values, out,
    meta, meta_all, own, recv, rhs, signs, sends, parts, full_a, full_b, w, w_cat,
    flips_v, source_v, offset_v, index_s,
    meta_s, meta_r, snap_s, snap_r, part_s, part_r, x_s, x_r, core_s, core_r, relay_s, relay_r, local_sem,
):
    group = n // 2
    rows = snap.shape[0]
    samples = parts.shape[2]
    tiles, nnz = tile_index.shape
    me, col = lax.axis_index("rows"), lax.axis_index("cols")
    place, first_row = me % group, me // group * group
    across, beside = flipped(col, 2), flipped(col, 1)

    local = [
        pltpu.make_async_copy(source, source_v, local_sem.at[0]),
        pltpu.make_async_copy(offset, offset_v, local_sem.at[1]),
        pltpu.make_async_copy(flips, flips_v, local_sem.at[2]),
        pltpu.make_async_copy(tile_index, index_s, local_sem.at[3]),
        pltpu.make_async_copy(
            snap.at[:, pl.ds(pl.multiple_of(place * TILE, TILE), TILE)], own, local_sem.at[4]
        ),
        pltpu.make_async_copy(tile_values, w, local_sem.at[5]),
    ]
    for copy in local:
        copy.start()

    barrier = pltpu.get_barrier_semaphore()
    for mask in range(1, n):
        pl.semaphore_signal(barrier, inc=1, device_id={"rows": flipped(me, mask)}, device_id_type=MESH)
    for other in (across, beside):
        pl.semaphore_signal(barrier, inc=1, device_id={"cols": other}, device_id_type=MESH)
    for copy in local[:3]:
        copy.wait()
    meta[...] = jnp.zeros_like(meta)
    meta[0:1, :] = source_v[...] * rows + offset_v[...]
    meta[1 : 1 + rows // LANES, :] = flips_v[...]
    meta_all[me] = meta[...]
    pl.semaphore_wait(barrier, n + 1)

    def meta_copy(mask):
        return pltpu.make_async_remote_copy(
            src_ref=meta, dst_ref=meta_all.at[me], send_sem=meta_s.at[mask], recv_sem=meta_r.at[mask],
            device_id={"rows": flipped(me, mask)}, device_id_type=MESH,
        )

    def snap_copy(q, mask):
        other = flipped(me, mask)
        start = pl.multiple_of((other % group) * TILE + q * LANES, LANES)
        return pltpu.make_async_remote_copy(
            src_ref=snap.at[:, pl.ds(start, LANES)], dst_ref=recv.at[q, place],
            send_sem=snap_s.at[q * group + mask], recv_sem=snap_r.at[q * group + mask],
            device_id={"rows": other}, device_id_type=MESH,
        )

    def part_copy(q, mask):
        return pltpu.make_async_remote_copy(
            src_ref=sends.at[q, mask], dst_ref=parts.at[q, me],
            send_sem=part_s.at[q * n + mask], recv_sem=part_r.at[q * n + mask],
            device_id={"rows": flipped(me, mask)}, device_id_type=MESH,
        )

    full = (full_a, full_b)

    def slot(c, mask):
        return c * group + flipped(me, mask) % group

    def col_copy(owner, q, mask, target, send, receive):
        at = slot(owner, mask)
        return pltpu.make_async_remote_copy(
            src_ref=full[q].at[at], dst_ref=full[q].at[at],
            send_sem=send.at[q * group + mask], recv_sem=receive.at[q * group + mask],
            device_id={"cols": target}, device_id_type=MESH,
        )

    x_copy = lambda q, mask: col_copy(col, q, mask, across, x_s, x_r)
    core_copy = lambda q, mask: col_copy(col, q, mask, beside, core_s, core_r)
    relay_copy = lambda q, mask: col_copy(across, q, mask, beside, relay_s, relay_r)

    for mask in range(n - 1, 0, -1):
        meta_copy(mask).start()
    for q in range(2):
        for mask in range(group - 1, 0, -1):
            snap_copy(q, mask).start()

    for mask in range(1, n):
        meta_copy(mask).wait_recv()
    lane = lax.broadcasted_iota(jnp.int32, (samples, LANES), 1)

    def folded(bits, width):
        while width > 1:
            width //= 2
            bits = bits ^ (bits >> width)
        return bits

    def owner_signs(d, carry):
        ids = jnp.broadcast_to(meta_all[d, 0:1, :], (samples, LANES)).T
        at = pl.ds(pl.multiple_of(d * samples, samples), samples)
        inner = [folded(ids & (lane + h * LANES), 16) for h in range(rows // LANES)]
        for g in range(group):
            outer = folded(ids & ((first_row + g) * rows), 16)
            for h in range(rows // LANES):
                parity = (inner[h] ^ outer ^ meta_all[first_row + g, 1 + h : 2 + h, :]) & 1
                begin = g * rows + h * LANES
                signs[at, begin : begin + LANES] = jnp.where(parity == 0, 1.0, -1.0).astype(jnp.bfloat16)
        return carry

    lax.fori_loop(0, n, owner_signs, 0)

    def put_rhs(q, g, block):
        hi, lo = split(block)
        at = pl.ds(pl.multiple_of(g * rows, rows), rows)
        rhs[q, at, 0:LANES] = hi
        rhs[q, at, LANES : 2 * LANES] = lo

    local[4].wait()
    for q in range(2):
        put_rhs(q, place, own[:, q * LANES : (q + 1) * LANES])

    def send_parts(q):
        for mask in range(1, group):
            snap_copy(q, mask).wait_recv()
            g = flipped(me, mask) % group
            put_rhs(q, g, recv[q, g])
        for mask in range(n - 1, -1, -1):
            d = flipped(me, mask)
            at = pl.ds(pl.multiple_of(d * samples, samples), samples)
            both = jnp.dot(signs[at, :], rhs[q], preferred_element_type=jnp.float32)
            ready = (both[:, :LANES] + both[:, LANES:]) * scale
            if mask:
                sends[q, mask] = ready
                part_copy(q, mask).start()
            else:
                parts[q, me] = ready

    send_parts(0)

    local[5].wait()

    def split_w(j, carry):
        for k in range(nnz):
            for q in range(2):
                hi, lo = split(w[j * nnz + k, q * LANES : (q + 1) * LANES, :])
                begin = 3 * k * LANES
                w_cat[q, j, begin : begin + LANES, :] = hi
                w_cat[q, j, begin + LANES : begin + 2 * LANES, :] = hi
                w_cat[q, j, begin + 2 * LANES : begin + 3 * LANES, :] = lo
        return carry

    lax.fori_loop(0, tiles, split_w, 0)

    send_parts(1)
    local[3].wait()

    for q in range(2):
        for mask in range(group):
            if mask:
                part_copy(q, mask).wait_recv()
            part_copy(q, mask + group).wait_recv()
            near, far = flipped(me, mask), flipped(me, mask + group)
            full[q][slot(col, mask)] = parts[q, near] + parts[q, far]
            x_copy(q, mask).start()
            core_copy(q, mask).start()
        for mask in range(group):
            col_copy(across, q, mask, across, x_s, x_r).wait_recv()
            relay_copy(q, mask).start()
        for mask in range(group):
            core_copy(q, mask).wait_recv()
            relay_copy(q, mask).wait_recv()
        for j in range(tiles):
            pieces = []
            for k in range(nnz):
                hi, lo = split(full[q][index_s[j, k]])
                pieces += [hi, lo, hi]
            sums = jnp.dot(jnp.concatenate(pieces, axis=1), w_cat[q, j], preferred_element_type=jnp.float32)
            at = slice(j * TILE, (j + 1) * TILE)
            out[:, at] = out[:, at] + sums if q else sums

    for mask in range(1, n):
        meta_copy(mask).wait_send()
    for q in range(2):
        for mask in range(1, n):
            part_copy(q, mask).wait_send()
        for mask in range(group):
            if mask:
                snap_copy(q, mask).wait_send()
            x_copy(q, mask).wait_send()
            core_copy(q, mask).wait_send()
            relay_copy(q, mask).wait_send()


def fused(snapshots, flips, sample_source, sample_offset, tile_index, tile_values):
    n, n_cols = lax.axis_size("rows"), lax.axis_size("cols")
    group = n // 2
    rows, width = snapshots.shape
    samples = sample_offset.shape[0]
    tiles, nnz = tile_index.shape
    weights = tile_values.reshape(tiles * nnz, TILE, TILE)
    scale = 1.0 / math.sqrt(samples * n)
    dma = lambda count: [pltpu.SemaphoreType.DMA((count,))] * 2
    return pl.pallas_call(
        functools.partial(kernel, n, scale),
        out_shape=jax.ShapeDtypeStruct((samples, width), jnp.float32),
        in_specs=[pl.BlockSpec(memory_space=pl.ANY)] * 6,
        out_specs=pl.BlockSpec(memory_space=pltpu.VMEM),
        scratch_shapes=[
            pltpu.VMEM((8, LANES), jnp.int32),
            pltpu.VMEM((n, 8, LANES), jnp.int32),
            pltpu.VMEM((rows, TILE), jnp.float32),
            pltpu.VMEM((2, group, rows, LANES), jnp.float32),
            pltpu.VMEM((2, group * rows, 2 * LANES), jnp.bfloat16),
            pltpu.VMEM((n * samples, group * rows), jnp.bfloat16),
            pltpu.VMEM((2, n, samples, LANES), jnp.float32),
            pltpu.VMEM((2, n, samples, LANES), jnp.float32),
            pltpu.VMEM((n_cols * group, samples, LANES), jnp.float32),
            pltpu.VMEM((n_cols * group, samples, LANES), jnp.float32),
            pltpu.VMEM((tiles * nnz, TILE, TILE), jnp.float32),
            pltpu.VMEM((2, tiles, 3 * nnz * LANES, TILE), jnp.bfloat16),
            pltpu.VMEM((rows // LANES, LANES), jnp.int32),
            pltpu.VMEM((1, LANES), jnp.int32),
            pltpu.VMEM((1, LANES), jnp.int32),
            pltpu.SMEM((tiles, nnz), jnp.int32),
        ]
        + dma(n) + dma(2 * group) + dma(2 * n) + dma(2 * group) + dma(2 * group) + dma(2 * group)
        + [pltpu.SemaphoreType.DMA((6,))],
        compiler_params=pltpu.CompilerParams(
            collective_id=0, has_side_effects=True, vmem_limit_bytes=60 * 2**20
        ),
    )(
        snapshots, flips.reshape(rows // LANES, LANES), sample_source.reshape(1, samples),
        sample_offset.reshape(1, samples), tile_index, weights,
    )


def on_device(snapshots, flips, sample_source, sample_offset, tile_index, tile_values):
    n, n_cols = lax.axis_size("rows"), lax.axis_size("cols")
    rows = snapshots.shape[0]
    fits = (
        n & (n - 1) == 0
        and 2 <= n <= 8
        and n_cols == 4
        and snapshots.shape[1] == n // 2 * TILE
        and rows & (rows - 1) == 0
        and LANES <= rows <= 4 * LANES
        and sample_offset.shape[0] == LANES
    )
    return (fused if fits else general)(
        snapshots, flips, sample_source, sample_offset, tile_index, tile_values
    )


def solution(mesh):
    return jax.shard_map(
        on_device,
        mesh=mesh,
        in_specs=(
            P("rows", "cols"),
            P("rows"),
            P("rows", None),
            P("rows"),
            P("cols", None),
            P("cols", None, None, None),
        ),
        out_specs=P("rows", "cols"),
        check_vma=False,
    )
```

time: 223 us -> 52.3 us (0.23)
  the two profiles are of different devices: /device:TPU:0 before, /device:TPU:5 now
where the time goes in v2:
time: 52.3 us; the launch traced here: 52.2 us
  Pallas kernels  50.3 us (96%)
  local copies, waits for them, and re-layouts  1.89 us (4%)
    pallas_call x1, Pallas kernels, fused(): pl.pallas_call(functools.partial(kernel, n, scale), out_shape=jax.ShapeDt...  50.3 us
    unnamed x1, local copies, waits for them, and re-layouts  1.89 us

profile of v2, /device:TPU:5, one launch (start us, length us, event | category | flops | bytes accessed | tf_op | source)
XLA Modules:
  0.0 52.2 jit_solution(6300021879313950211)
XLA Ops:
  0.0 50.3 %shard_map.64 = f32[128,1024]{1,0:T(8,128)} custom-call(f32[256,1024]{1,0:T(8,128)} %snap.1, s32[2,128]{1,0:T(2,128)} %bitcast.5, s32[1,128]{1,0:T(1,128)} %bitcast.6, s32[1,128]{1,0:T(1,128)} %bitcast.7, s32[4,3]{1,0:T(4,128)} %tile_index.1, f32[12,256,256]{2,1,0:T(8,128)} %bitcast.4), custom_call_target="tpu_custom_call" | custom-call | tf_op jit(solution)/shard_map/pallas_call | solution.py:300
  50.3 1.9 %copy.8 = f32[128,1024]{1,0:T(8,128)} copy(f32[128,1024]{1,0:T(8,128)} %shard_map.64) | data formatting | bytes 1048576

commit v3 on v2

--- a/solution.py
+++ b/solution.py
@@ -12,6 +12,7 @@
 LANES = 128
 MESH = pl.DeviceIdType.MESH
 HIGHEST = lax.Precision.HIGHEST
+WINDOW = 5
 
 
 def swapped(array, axis, bit):
@@ -178,9 +179,8 @@
 
     for mask in range(n - 1, 0, -1):
         meta_copy(mask).start()
-    for q in range(2):
-        for mask in range(group - 1, 0, -1):
-            snap_copy(q, mask).start()
+    for mask in range(group - 1, 0, -1):
+        snap_copy(0, mask).start()
 
     for mask in range(1, n):
         meta_copy(mask).wait_recv()
@@ -216,23 +216,45 @@
     for q in range(2):
         put_rhs(q, place, own[:, q * LANES : (q + 1) * LANES])
 
-    def send_parts(q):
+    def arrive(q):
         for mask in range(1, group):
             snap_copy(q, mask).wait_recv()
             g = flipped(me, mask) % group
             put_rhs(q, g, recv[q, g])
-        for mask in range(n - 1, -1, -1):
-            d = flipped(me, mask)
-            at = pl.ds(pl.multiple_of(d * samples, samples), samples)
-            both = jnp.dot(signs[at, :], rhs[q], preferred_element_type=jnp.float32)
-            ready = (both[:, :LANES] + both[:, LANES:]) * scale
-            if mask:
-                sends[q, mask] = ready
-                part_copy(q, mask).start()
-            else:
-                parts[q, me] = ready
-
-    send_parts(0)
+
+    def part(q, mask):
+        at = pl.ds(pl.multiple_of(flipped(me, mask) * samples, samples), samples)
+        both = jnp.dot(signs[at, :], rhs[q], preferred_element_type=jnp.float32)
+        return (both[:, :LANES] + both[:, LANES:]) * scale
+
+    order = [group] + [m for i in range(1, group) for m in (i, group + i)]
+    queue = [(q, mask) for q in range(2) for mask in order]
+
+    def send_part(at):
+        q, mask = queue[at]
+        sends[q, mask] = part(q, mask)
+        if at >= WINDOW:
+            part_copy(*queue[at - WINDOW]).wait_send()
+        part_copy(q, mask).start()
+
+    def piece(q, mask):
+        if mask:
+            part_copy(q, mask).wait_recv()
+        part_copy(q, mask + group).wait_recv()
+        full[q][slot(col, mask)] = parts[q, flipped(me, mask)] + parts[q, flipped(me, mask + group)]
+        x_copy(q, mask).start()
+        core_copy(q, mask).start()
+
+    def relay(q, mask):
+        col_copy(across, q, mask, across, x_s, x_r).wait_recv()
+        relay_copy(q, mask).start()
+
+    arrive(0)
+    for mask in range(group - 1, 0, -1):
+        snap_copy(1, mask).start()
+    for at in range(WINDOW):
+        send_part(at)
+    parts[0, me] = part(0, 0)
 
     local[5].wait()
 
@@ -248,21 +270,22 @@
 
     lax.fori_loop(0, tiles, split_w, 0)
 
-    send_parts(1)
+    for at in range(WINDOW, len(order)):
+        send_part(at)
     local[3].wait()
-
-    for q in range(2):
-        for mask in range(group):
-            if mask:
-                part_copy(q, mask).wait_recv()
-            part_copy(q, mask + group).wait_recv()
-            near, far = flipped(me, mask), flipped(me, mask + group)
-            full[q][slot(col, mask)] = parts[q, near] + parts[q, far]
-            x_copy(q, mask).start()
-            core_copy(q, mask).start()
-        for mask in range(group):
-            col_copy(across, q, mask, across, x_s, x_r).wait_recv()
-            relay_copy(q, mask).start()
+    arrive(1)
+    todo = [(piece, mask) for mask in range(group)] + [(relay, mask) for mask in range(group)]
+    for at in range(len(order)):
+        send_part(len(order) + at)
+        if at == 0:
+            parts[1, me] = part(1, 0)
+        else:
+            step, mask = todo.pop(0)
+            step(0, mask)
+    for step, mask in todo:
+        step(0, mask)
+
+    def incidence(q):
         for mask in range(group):
             core_copy(q, mask).wait_recv()
             relay_copy(q, mask).wait_recv()
@@ -275,11 +298,19 @@
             at = slice(j * TILE, (j + 1) * TILE)
             out[:, at] = out[:, at] + sums if q else sums
 
+    incidence(0)
+    for mask in range(group):
+        piece(1, mask)
+        if mask:
+            relay(1, mask - 1)
+    relay(1, group - 1)
+    incidence(1)
+
     for mask in range(1, n):
         meta_copy(mask).wait_send()
+    for copy in queue[-WINDOW:]:
+        part_copy(*copy).wait_send()
     for q in range(2):
-        for mask in range(1, n):
-            part_copy(q, mask).wait_send()
         for mask in range(group):
             if mask:
                 snap_copy(q, mask).wait_send()

time: 52.3 us -> 49.1 us (0.939)
  the two profiles are of different devices: /device:TPU:5 before, /device:TPU:0 now
where the time goes in v3:
time: 49.1 us; the launch traced here: 48.9 us
  Pallas kernels  47 us (96%)
  local copies, waits for them, and re-layouts  1.89 us (4%)
    pallas_call x1, Pallas kernels, fused(): pl.pallas_call(functools.partial(kernel, n, scale), out_shape=jax.ShapeDt...  47 us
    unnamed x1, local copies, waits for them, and re-layouts  1.89 us

profile of v3, /device:TPU:0, one launch (start us, length us, event | category | flops | bytes accessed | tf_op | source)
XLA Modules:
  0.0 48.9 jit_solution(18439525436588008782)
XLA Ops:
  0.0 47.0 %shard_map.64 = f32[128,1024]{1,0:T(8,128)} custom-call(f32[256,1024]{1,0:T(8,128)} %snap.1, s32[2,128]{1,0:T(2,128)} %bitcast.5, s32[1,128]{1,0:T(1,128)} %bitcast.6, s32[1,128]{1,0:T(1,128)} %bitcast.7, s32[4,3]{1,0:T(4,128)} %tile_index.1, f32[12,256,256]{2,1,0:T(8,128)} %bitcast.4), custom_call_target="tpu_custom_call" | custom-call | tf_op jit(solution)/shard_map/pallas_call | solution.py:331
  47.0 1.9 %copy.8 = f32[128,1024]{1,0:T(8,128)} copy(f32[128,1024]{1,0:T(8,128)} %shard_map.64) | data formatting | bytes 1048576
